TPU v7x, 768 devices: a whole 4x8x12 slice. The times are simulated.
768 devices in a mesh: row: 32 (over y_hi, x, core), col: 24 (over z, y_lo).
Axes of the slice: x: 4, y: 8 (y_hi: 4, y_lo: 2; y = y_hi * 2 + y_lo), z: 12, core: 2. Of those that a mesh axis runs over, the one named last changes fastest.
Arguments:
- tiles: bfloat16 [32, 24, 128, 128, 128], P('row', 'col'), may hold values from -0.09375 to 0.09375
- tile_row: int32 [32, 24, 128], P('row', 'col'), may hold values from 0 to 191
- tile_col: int32 [32, 24, 128], P('row', 'col'), may hold values from 0 to 255
- basis: float32 [8, 786432], P(None, ('row', 'col')), may hold values from -240 to 240
- basis_image: float32 [8, 786432], P(None, ('row', 'col')), may hold values from -240 to 240
- search: float32 [8, 786432], P(None, ('row', 'col')), may hold values from -240 to 240
- search_image: float32 [8, 786432], P(None, ('row', 'col')), may hold values from -240 to 240
- ritz_values: float32 [8], replicated, may hold values from -3 to 3
Outputs:
- ritz_basis: float32 [24, 786432], P(None, ('row', 'col'))
- ritz_images: float32 [24, 786432], P(None, ('row', 'col'))
- projected: float32 [24, 24], replicated
All inputs are finite; a program needn't handle non-finite values.
Results may differ from a plain program's by a relative error of at most 0.0021.
Values may be sent and summed in bfloat16 or wider, within the bound.
A program may use at most 32 MiB of HBM per device.

v0:
```python
import jax
import jax.numpy as jnp
from jax import lax
from jax.sharding import PartitionSpec as P

TILE = 128
VECS = 8


def factor(gram):
    size = gram.shape[0]
    lower = jnp.zeros_like(gram)
    index = jnp.arange(size)
    for step in range(size):
        column = gram[:, step] - jnp.sum(lower * lower[step][None, :], axis=1)
        pivot = jnp.sqrt(column[step])
        column = jnp.where(index >= step, column / pivot, jnp.float32(0.0))
        lower = lower.at[:, step].set(column)
    return lower


def invert(lower):
    size = lower.shape[0]
    identity = jnp.eye(size, dtype=lower.dtype)
    inverse = jnp.zeros_like(lower)
    for step in range(size):
        solved = (identity[step] - jnp.sum(lower[step][:, None] * inverse, axis=0)) / lower[
            step, step
        ]
        inverse = inverse.at[step].set(solved)
    return inverse


def product(left, right):
    return jnp.dot(left, right.T, precision=lax.Precision.HIGHEST)


def place(values, index, count, start):
    onehot = (index[None, :] - start == jnp.arange(count, dtype=jnp.int32)[:, None]).astype(
        jnp.float32
    )
    return jnp.einsum("nk,kvi->nvi", onehot, values, precision=lax.Precision.HIGHEST)


def on_device(tiles, tile_row, tile_col, basis, basis_image, search, search_image, ritz_values):
    n_total = basis.shape[1] * lax.axis_size("row") * lax.axis_size("col")
    residual = basis_image - ritz_values[:, None] * basis
    stack = jnp.concatenate([basis, residual, search], axis=0)
    lowered = residual.astype(jnp.bfloat16)
    col_inputs = lax.all_gather(lowered, "row", axis=1, tiled=True)
    row_inputs = lax.all_gather(lowered, "col", axis=1, tiled=True)
    blocks = tiles[0, 0]
    rows = tile_row[0, 0]
    cols = tile_col[0, 0]
    picked_cols = col_inputs.reshape(VECS, -1, TILE)[:, cols]
    picked_rows = row_inputs.reshape(VECS, -1, TILE)[:, rows]
    forward = jnp.einsum("kij,vkj->kvi", blocks, picked_cols, preferred_element_type=jnp.float32)
    backward = jnp.einsum("kij,vki->kvj", blocks, picked_rows, preferred_element_type=jnp.float32)
    row_terms = place(forward, rows, row_inputs.shape[1] // TILE, 0)
    summed = lax.psum_scatter(row_terms, "col", scatter_dimension=0, tiled=True)
    col_terms = place(backward, cols, col_inputs.shape[1] // TILE, 0)
    summed = summed + lax.psum_scatter(col_terms, "row", scatter_dimension=0, tiled=True)
    residual_image = summed.transpose(1, 0, 2).reshape(VECS, -1)
    images = jnp.concatenate([basis_image, residual_image, search_image], axis=0)
    gram_total, raw_total = lax.psum(
        (product(stack, stack), product(stack, images)), ("row", "col")
    )
    gram = gram_total / n_total
    raw = raw_total / n_total
    inverse = invert(factor(gram))
    highest = lax.Precision.HIGHEST
    ritz_basis = jnp.dot(inverse, stack, precision=highest)
    ritz_images = jnp.dot(inverse, images, precision=highest)
    projected = jnp.dot(jnp.dot(inverse, raw, precision=highest), inverse.T, precision=highest)
    return (ritz_basis, ritz_images, projected)


def solution(mesh):
    return jax.shard_map(
        on_device,
        mesh=mesh,
        in_specs=(
            P("row", "col", None, None, None),
            P("row", "col", None),
            P("row", "col", None),
            P(None, ("row", "col")),
            P(None, ("row", "col")),
            P(None, ("row", "col")),
            P(None, ("row", "col")),
            P(),
        ),
        out_specs=(P(None, ("row", "col")), P(None, ("row", "col")), P()),
        check_vma=False,
    )
```

profile of v0, /device:TPU:1, one launch (start us, length us, event | category | flops | bytes accessed | tf_op | source)
XLA Modules:
  0.0 489.1 jit_solution(15921769236033065476)
XLA Ops:
  8.1 50.2 %all_gather.7 = bf16[8,24576]{1,0:T(8,128)(2,1)S(1)} all-gather(bf16[8,1024]{1,0:T(8,128)(2,1)S(1)} %get-tuple-element.604), channel_id=1, replica_groups=mesh['row'=32,'col'=24] {'col'}, dimensions={1}, use_global_device_ids=true | all-gather | bytes 409600 | tf_op jit(solution)/shard_map/all_gather | solution.py:51
  59.6 3.4 fusion
  63.0 1.6 fusion.4
  64.8 56.9 %all_gather.6 = bf16[8,32768]{1,0:T(8,128)(2,1)S(1)} all-gather(bf16[8,1024]{1,0:T(8,128)(2,1)S(1)} %get-tuple-element.604), channel_id=1, replica_groups=mesh['row'=32,'col'=24] {'row'}, dimensions={1}, use_global_device_ids=true | all-gather | bytes 540672 | tf_op jit(solution)/shard_map/all_gather | solution.py:50
  122.4 4.4 fusion.2
  126.8 1.5 fusion.6
  144.0 28.4 %reduce-scatter.5.cloned.1.call-done = f32[8,8,128]{2,0,1:T(8,128)} async-done(((f32[256,8,128]{2,0,1:T(8,128)}), f32[8,8,128]{2,0,1:T(8,128)}) %reduce-scatter.5.cloned.1.call-update) | async-done | bytes 32784 | tf_op jit(solution)/shard_map/reduce_scatter | solution.py:62
  172.3 92.6 %reduce-scatter.3.cloned.1.call-done = f32[8,8,128]{2,0,1:T(8,128)} async-done(((f32[192,8,128]{2,0,1:T(8,128)}), f32[8,8,128]{2,0,1:T(8,128)}) %reduce-scatter.3.cloned.1.call-update) | async-done | bytes 32784 | tf_op jit(solution)/shard_map/reduce_scatter | solution.py:60
  266.0 123.6 %all-reduce.2 = (f32[24,24]{1,0:T(8,128)S(1)}, f32[24,24]{1,0:T(8,128)S(1)}) all-reduce(f32[24,24]{1,0:T(8,128)S(1)} %fusion.18, f32[24,24]{1,0:T(8,128)S(1)} %fusion.16), channel_id=1, replica_groups=mesh['row'=32,'col'=24] {'row','col'}, use_global_device_ids=true, to_apply=%region_1.0 | all-reduce | flops 1152 | bytes 9216 | tf_op jit(solution)/shard_map/psum | solution.py:65
  452.4 1.4 fusion.44
  453.9 1.4 fusion.43
  456.7 1.3 fusion.41
  458.2 1.3 fusion.40
  459.6 1.3 fusion.39
  462.4 1.3 fusion.37
  463.9 1.3 fusion.36
  465.3 1.3 fusion.35
  466.8 1.3 fusion.34
  468.2 1.4 fusion.33
  471.1 1.4 fusion.31
  474.0 1.3 fusion.29
  475.4 1.3 fusion.28
  476.8 1.3 fusion.27
  478.3 1.3 fusion.26
  (281 shorter events, 75.0 us)
Async XLA Ops:
  7.2 55.9 %copy-start.4 = (s32[1,1,128]{2,1,0:T(1,128)S(1)}, s32[1,1,128]{2,1,0:T(1,128)}, u32[]{:S(2)}) copy-start(s32[1,1,128]{2,1,0:T(1,128)} %param.106) | copy-start | bytes 1540
  7.2 165.2 %reduce-scatter.5.cloned.1.call-start = ((), (), s32[]{:S(2)}) async-start(), calls=%async_computation.3 | async-start | bytes 1081344 | tf_op jit(solution)/shard_map/reduce_scatter | solution.py:62
  63.0 63.8 %copy-start.5 = (s32[1,1,128]{2,1,0:T(1,128)S(1)}, s32[1,1,128]{2,1,0:T(1,128)}, u32[]{:S(2)}) copy-start(s32[1,1,128]{2,1,0:T(1,128)} %param.105) | copy-start | bytes 1540
  64.7 79.1 %copy-start = (f32[8,1024]{1,0:T(8,128)S(1)}, f32[8,1024]{1,0:T(8,128)}, u32[]{:S(2)}) copy-start(f32[8,1024]{1,0:T(8,128)} %param.107) | copy-start | bytes 98308
  64.7 79.1 %copy-start.1 = (f32[8,1024]{1,0:T(8,128)S(1)}, f32[8,1024]{1,0:T(8,128)}, u32[]{:S(2)}) copy-start(f32[8,1024]{1,0:T(8,128)} %param.109) | copy-start | bytes 98308
  64.7 200.3 %reduce-scatter.3.cloned.1.call-start = ((), (), s32[]{:S(2)}) async-start(), calls=%async_computation.2 | async-start | bytes 819200 | tf_op jit(solution)/shard_map/reduce_scatter | solution.py:60
  64.8 201.0 %copy-start.3 = (f32[8,1024]{1,0:T(8,128)S(1)}, f32[8,1024]{1,0:T(8,128)}, u32[]{:S(2)}) copy-start(f32[8,1024]{1,0:T(8,128)} %param.110) | copy-start | bytes 98308
  143.7 307.3 %copy-start.2 = (f32[24,24]{1,0:T(8,128)}, f32[24,24]{1,0:T(8,128)S(1)}, u32[]{:S(2)}) copy-start(f32[24,24]{1,0:T(8,128)S(1)} %fusion.22) | copy-start | bytes 6916
Sparse Core Ops, SparseCore 0:
  64.8 107.5 reduce-scatter.4
  175.7 89.2 reduce-scatter.2
where the time goes:
time: 491 us; the launch traced here: 489 us
  blocking collectives  231 us (47%)
  waiting for transfers between devices  121 us (25%)
  other arithmetic  68.6 us (14%)
  between operations  31.3 us (6%)
  local copies, waits for them, and re-layouts  23.3 us (5%)
  matrix products  14 us (3%)
    psum x1, blocking collectives, on_device(): lax.psum((product(stack, stack), product(stack, images)), ('row', 'col'))  124 us
    reduce_scatter x1, waiting for transfers between devices, on_device(): summed = lax.psum_scatter(row_terms, 'col', scatter_dimension=0, tiled=True)  92.6 us
    all_gather x1, blocking collectives, on_device(): col_inputs = lax.all_gather(lowered, 'row', axis=1, tiled=True)  56.9 us
    all_gather x1, blocking collectives, on_device(): row_inputs = lax.all_gather(lowered, 'col', axis=1, tiled=True)  50.2 us
    another operation x45, other arithmetic  30.5 us
    div x24, other arithmetic, invert(): (identity[step] - jnp.sum(lower[step][:, None] * inverse, axis=0)) / lowe...  29.5 us
    reduce_scatter x1, waiting for transfers between devices, on_device(): lax.psum_scatter(col_terms, 'row', scatter_dimension=0, tiled=True)  28.4 us
    slice x24, local copies, waits for them, and re-layouts, factor(): pivot = jnp.sqrt(column[step])  14 us
  transfers between devices with their start and end apart: 2, of which 2 were waited for; matrix products, arithmetic and copies ran while one was open for 5% of the time, Pallas kernels for 0%

commit v1 on v0

v1 whole, which is shorter than its diff:
```python
import jax
import jax.numpy as jnp
from jax import lax
from jax.experimental import pallas as pl
from jax.experimental.pallas import tpu as pltpu
from jax.sharding import PartitionSpec as P

MESH = pl.DeviceIdType.MESH
TILE = 128
VECS = 8
TILES = 128
N_YH, N_X, N_Z = 4, 4, 12
N_XY = N_YH * N_X
N_ROW, N_COL = 2 * N_XY, 2 * N_Z
F32 = jnp.float32
BF16 = jnp.bfloat16
HIGHEST = lax.Precision.HIGHEST
NT = (((1,), (1,)), ((), ()))
NN = (((1,), (0,)), ((), ()))


def dot_nt(left, right):
    return lax.dot_general(left, right, NT, precision=HIGHEST, preferred_element_type=F32)


def dot_nn(left, right):
    return lax.dot_general(left, right, NN, precision=HIGHEST, preferred_element_type=F32)


def slots_of(index, groups):
    piece, within = index // 8, index % 8
    return ((piece % 2) * groups + piece // 2) * 8 + within


def onehots(ahead, across, slots, count):
    column = jnp.transpose(jnp.broadcast_to(slots.astype(F32), (TILES, TILES)))
    lane = lax.broadcasted_iota(jnp.int32, (TILES, count), 1).astype(F32)
    ahead[...] = (lane == jnp.concatenate([column, column], axis=1)[:, :count]).astype(F32).astype(BF16)
    across[...] = (lax.broadcasted_iota(jnp.int32, (count, TILES), 0) == slots).astype(F32).astype(BF16)


def pick(picked, pieces, ahead, count):
    for m in range(VECS // 2):
        pair = pieces[:, 16 * m:16 * m + 16, :].astype(F32)
        even = pair[:, 0:8, :].reshape(count, TILE).astype(BF16)
        odd = pair[:, 8:16, :].reshape(count, TILE).astype(BF16)
        chosen = lax.dot_general(
            ahead[...], jnp.concatenate([even, odd], axis=1), NN, preferred_element_type=F32
        )
        picked[pl.ds(2 * m, TILES, stride=VECS), :] = chosen[:, :TILE]
        picked[pl.ds(2 * m + 1, TILES, stride=VECS), :] = chosen[:, TILE:]


def place(terms, products, across, count):
    left = jnp.concatenate([across[...], across[...]], axis=1)
    for v in range(0, VECS, 2):
        columns = []
        for u in (v, v + 1):
            values = products[pl.ds(u, TILES, stride=VECS), :]
            high = values.astype(BF16)
            low = (values - high.astype(F32)).astype(BF16)
            columns.append(jnp.concatenate([high, low], axis=0))
        total = lax.dot_general(
            left, jnp.concatenate(columns, axis=1), NN, preferred_element_type=F32
        )
        terms[:, 8 * v:8 * v + 8, :] = total[:, :TILE].reshape(count // 8, 8, TILE)
        terms[:, 8 * v + 8:8 * v + 16, :] = total[:, TILE:].reshape(count // 8, 8, TILE)


def kernel(
    tiles_hbm, row_hbm, col_hbm, basis_hbm, image_hbm, search_hbm, simage_hbm, ritz_hbm,
    ob_hbm, oi_hbm, op_hbm,
    tiles, row_v, col_v, ritz_s, work, images, pieces,
    ahead_r, across_r, ahead_c, across_c, picked_f, picked_b,
    colbuf, rowbuf, products_f, products_b, rowterms, colterms, rowlow, zr, zs, yr,
    csib, csum, cr, ob, oi, opv,
    g_core, g_xy, g_yl, g_z, l_core, l_xy, l_yl, l_z,
    in_sem, out_sem,
    cA_s, cA_r, cB_s, cB_r, zA_s, zA_r, yB_s, yB_r,
    rz_s, rz_r, ry_s, ry_r, sc_s, sc_r, sx_s, sx_r,
    gc_s, gc_r, gx_s, gx_r, gy_s, gy_r, gz_s, gz_r,
    lc_s, lc_r, lx_s, lx_r, ly_s, ly_r, lz_s, lz_r,
):
    row = lax.axis_index("row")
    col = lax.axis_index("col")
    xy, core = row // 2, row % 2
    yh, x = xy // N_X, xy % N_X
    z, yl = col // 2, col % 2
    sibling = (xy * 2 + 1 - core, col)
    across = (row, z * 2 + 1 - yl)

    def plane(dy, dx):
        return (((yh + dy) % N_YH) * N_X + (x + dx) % N_X)

    def plane_from(dy, dx):
        return (((yh + N_YH - dy) % N_YH) * N_X + (x + N_X - dx) % N_X)

    offsets = [(dy, dx) for dy in range(N_YH) for dx in range(N_X)][1:]
    z_order = [6, 5, 7, 4, 8, 3, 9, 2, 10, 1, 11]

    def z_peer(d):
        return (row, ((z + d) % N_Z) * 2 + yl)

    def xy_peer(o):
        return (plane(*o) * 2 + core, col)

    barrier = pltpu.get_barrier_semaphore()
    everyone = [z_peer(d) for d in z_order] + [xy_peer(o) for o in offsets] + [sibling, across]
    for peer in everyone:
        pl.semaphore_signal(barrier, inc=1, device_id=peer, device_id_type=MESH)

    loads = [
        pltpu.make_async_copy(basis_hbm, work.at[pl.ds(0, 8)], in_sem.at[0]),
        pltpu.make_async_copy(image_hbm, work.at[pl.ds(24, 8)], in_sem.at[1]),
        pltpu.make_async_copy(ritz_hbm, ritz_s, in_sem.at[2]),
        pltpu.make_async_copy(search_hbm, work.at[pl.ds(16, 8)], in_sem.at[3]),
        pltpu.make_async_copy(simage_hbm, work.at[pl.ds(32, 8)], in_sem.at[4]),
        pltpu.make_async_copy(row_hbm, row_v, in_sem.at[5]),
        pltpu.make_async_copy(col_hbm, col_v, in_sem.at[6]),
        pltpu.make_async_copy(tiles_hbm.at[0, 0], tiles, in_sem.at[7]),
    ]
    for load in loads:
        load.start()
    for load in loads[:3]:
        load.wait()
    v_index = lax.broadcasted_iota(jnp.int32, (VECS, 1), 0)
    ritz = jnp.zeros((VECS, 1), F32)
    for v in range(VECS):
        ritz = jnp.where(v_index == v, ritz_s[v], ritz)
    residual = work[24:32, :] - ritz * work[0:8, :]
    work[8:16, :] = residual
    mine_col = core * N_XY + xy
    mine_row = yl * N_Z + z
    for t in range(8):
        pieces[pl.ds(t, VECS, stride=8), :] = residual[:, t * TILE:(t + 1) * TILE]
    lowered = pieces[...].astype(BF16)
    colbuf[mine_col] = lowered
    rowbuf[mine_row] = lowered

    pl.semaphore_wait(barrier, len(everyone))

    sends = []

    def remote(src, dst, ss, rs, peer):
        copy = pltpu.make_async_remote_copy(
            src_ref=src, dst_ref=dst, send_sem=ss, recv_sem=rs, device_id=peer, device_id_type=MESH
        )
        return copy

    def send(src, dst, ss, rs, peer):
        copy = remote(src, dst, ss, rs, peer)
        copy.start()
        sends.append(copy)

    def arrived(dst, ss, rs, peer):
        remote(dst, dst, ss, rs, peer).wait_recv()

    for d in z_order:
        send(rowbuf.at[mine_row], rowbuf.at[mine_row], zA_s.at[d], zA_r.at[d], z_peer(d))
    for j, o in enumerate(offsets):
        send(colbuf.at[mine_col], colbuf.at[mine_col], cA_s.at[j], cA_r.at[j], xy_peer(o))
    send(rowbuf.at[mine_row], rowbuf.at[mine_row], yB_s.at[0], yB_r.at[0], across)

    for load in loads[5:7]:
        load.wait()
    onehots(ahead_r, across_r, slots_of(row_v[0], N_Z), N_COL * 8)
    onehots(ahead_c, across_c, slots_of(col_v[0], N_XY), N_ROW * 8)

    for load in loads[3:5]:
        load.wait()
    g_core[core] = jnp.zeros((24, TILE), F32)
    g_core[core, :, 0:40] = dot_nt(work[0:24, :], work[0:40, :])
    send(g_core.at[core], g_core.at[core], gc_s, gc_r, sibling)

    for dy in range(N_YH):
        base = core * N_XY + ((yh + N_YH - dy) % N_YH) * N_X
        for dx in range(N_X):
            if (dy, dx) != (0, 0):
                j = offsets.index((dy, dx))
                here = colbuf.at[core * N_XY + plane_from(dy, dx)]
                arrived(here, cA_s.at[j], cA_r.at[j], xy_peer((dy, dx)))
        block = colbuf.at[pl.ds(base, N_X)]
        send(block, block, cB_s.at[dy], cB_r.at[dy], sibling)
    for d in reversed(z_order):
        here = rowbuf.at[yl * N_Z + (z + N_Z - d) % N_Z]
        arrived(here, zA_s.at[d], zA_r.at[d], z_peer(d))
        send(here, here, yB_s.at[d], yB_r.at[d], across)

    arrived(g_core.at[1 - core], gc_s, gc_r, sibling)
    g_xy[xy] = g_core[0] + g_core[1]
    for j, o in enumerate(offsets):
        send(g_xy.at[xy], g_xy.at[xy], gx_s.at[j], gx_r.at[j], xy_peer(o))

    for dy in range(N_YH):
        block = colbuf.at[pl.ds((1 - core) * N_XY + ((yh + N_YH - dy) % N_YH) * N_X, N_X)]
        arrived(block, cB_s.at[dy], cB_r.at[dy], sibling)
    loads[7].wait()

    def forward(step, carry):
        for u in range(8):
            k = step * 8 + u
            at = pl.ds(pl.multiple_of(k * 8, 8), 8)
            products_f[at, :] = lax.dot_general(
                picked_f[at, :].astype(BF16), tiles[k], NT, preferred_element_type=F32
            )
        return carry

    pick(picked_f, colbuf, ahead_c, N_ROW * 8)
    lax.fori_loop(0, TILES // 8, forward, 0)
    place(rowterms, products_f, across_r, N_COL * 8)
    rowlow[...] = rowterms[...].astype(BF16)
    for h, d in [(h, d) for h in (0, 1) for d in z_order]:
        send(
            rowlow.at[h * N_Z + (z + d) % N_Z], zr.at[h, z], rz_s.at[h, d], rz_r.at[h, d], z_peer(d)
        )

    for j, o in enumerate(offsets):
        arrived(g_xy.at[plane_from(*o)], gx_s.at[j], gx_r.at[j], xy_peer(o))
    total = g_xy[0]
    for j in range(1, N_XY):
        total = total + g_xy[j]
    g_yl[yl] = total
    send(g_yl.at[yl], g_yl.at[yl], gy_s, gy_r, across)

    for d in range(N_Z):
        here = rowbuf.at[(1 - yl) * N_Z + (z + N_Z - d) % N_Z]
        arrived(here, yB_s.at[d], yB_r.at[d], across)

    def backward(step, carry):
        for u in range(8):
            k = step * 8 + u
            at = pl.ds(pl.multiple_of(k * 8, 8), 8)
            products_b[at, :] = lax.dot_general(
                picked_b[at, :].astype(BF16), tiles[k], NN, preferred_element_type=F32
            )
        return carry

    pick(picked_b, rowbuf, ahead_r, N_COL * 8)
    lax.fori_loop(0, TILES // 8, backward, 0)
    place(colterms, products_b, across_c, N_ROW * 8)

    chunk = N_XY // 4
    for q in range(4):
        send(
            colterms.at[pl.ds((1 - core) * N_XY + q * chunk, chunk)],
            csib.at[pl.ds(q * chunk, chunk)], sc_s.at[q], sc_r.at[q], sibling,
        )
    arrived(g_yl.at[1 - yl], gy_s, gy_r, across)
    g_z[z] = g_yl[0] + g_yl[1]
    for d in z_order:
        send(g_z.at[z], g_z.at[z], gz_s.at[d], gz_r.at[d], z_peer(d))
    for q in range(4):
        arrived(csib.at[pl.ds(q * chunk, chunk)], sc_s.at[q], sc_r.at[q], sibling)
    for q in range(N_XY):
        csum[q] = (colterms[core * N_XY + q] + csib[q]).astype(BF16)
    for j, o in enumerate(offsets):
        send(csum.at[plane(*o)], cr.at[xy], sx_s.at[j], sx_r.at[j], xy_peer(o))

    for h, d in [(h, d) for h in (0, 1) for d in z_order]:
        arrived(zr.at[h, (z + N_Z - d) % N_Z], rz_s.at[h, d], rz_r.at[h, d], z_peer(d))

    def over_z(h):
        total = rowterms[h * N_Z + z]
        for d in range(1, N_Z):
            total = total + zr[h, (z + d) % N_Z].astype(F32)
        return total

    zs[0] = over_z(1 - yl)
    send(zs.at[0], yr, ry_s, ry_r, across)
    zs[1] = over_z(yl)

    for d in z_order:
        arrived(g_z.at[(z + N_Z - d) % N_Z], gz_s.at[d], gz_r.at[d], z_peer(d))
    total = g_z[0]
    for j in range(1, N_Z):
        total = total + g_z[j]
    n_total = F32(1024 * N_ROW * N_COL)
    total = total / n_total
    rows = lax.broadcasted_iota(jnp.int32, (24, 24), 0)
    columns = lax.broadcasted_iota(jnp.int32, (24, 24), 1)
    matrix = jnp.concatenate([total[:, 0:24], jnp.where(rows == columns, F32(1.0), F32(0.0))], axis=1)
    index = lax.broadcasted_iota(jnp.int32, (24, 1), 0)
    for step in range(24):
        pivot = jnp.sqrt(matrix[step:step + 1, step:step + 1])
        scaled = matrix[step:step + 1, :] / pivot
        factor = matrix[:, step:step + 1] / pivot
        matrix = jnp.where(
            index == step, scaled, jnp.where(index > step, matrix - factor * scaled, matrix)
        )
    inverse = matrix[:, 24:48]
    given = dot_nt(dot_nn(inverse, total[:, 24:32]), inverse[:, 0:8]) + dot_nt(
        dot_nn(inverse, total[:, 32:40]), inverse[:, 16:24]
    )
    ob[...] = dot_nn(inverse, work[0:24, :])
    store_b = pltpu.make_async_copy(ob, ob_hbm, out_sem.at[0])
    store_b.start()

    arrived(yr, ry_s, ry_r, across)
    image = zs[1] + yr[...] + (colterms[core * N_XY + xy] + csib[xy])
    for j, o in enumerate(offsets):
        here = cr.at[plane_from(*o)]
        arrived(here, sx_s.at[j], sx_r.at[j], xy_peer(o))
        image = image + cr[plane_from(*o)].astype(F32)
    pieces[...] = image
    for t in range(8):
        images[8:16, t * TILE:(t + 1) * TILE] = pieces[pl.ds(t, VECS, stride=8), :]
    images[0:8, :] = work[24:32, :]
    images[16:24, :] = work[32:40, :]

    l_core[core] = jnp.zeros((VECS, TILE), F32)
    l_core[core, :, 0:24] = dot_nt(images[8:16, :], work[0:24, :])
    send(l_core.at[core], l_core.at[core], lc_s, lc_r, sibling)
    arrived(l_core.at[1 - core], lc_s, lc_r, sibling)
    l_xy[xy] = l_core[0] + l_core[1]
    for j, o in enumerate(offsets):
        send(l_xy.at[xy], l_xy.at[xy], lx_s.at[j], lx_r.at[j], xy_peer(o))
    oi[...] = dot_nn(inverse, images[...])
    store_i = pltpu.make_async_copy(oi, oi_hbm, out_sem.at[1])
    store_i.start()
    for j, o in enumerate(offsets):
        arrived(l_xy.at[plane_from(*o)], lx_s.at[j], lx_r.at[j], xy_peer(o))
    late = l_xy[0]
    for j in range(1, N_XY):
        late = late + l_xy[j]
    l_yl[yl] = late
    send(l_yl.at[yl], l_yl.at[yl], ly_s, ly_r, across)
    arrived(l_yl.at[1 - yl], ly_s, ly_r, across)
    l_z[z] = l_yl[0] + l_yl[1]
    for d in z_order:
        send(l_z.at[z], l_z.at[z], lz_s.at[d], lz_r.at[d], z_peer(d))
    for d in z_order:
        arrived(l_z.at[(z + N_Z - d) % N_Z], lz_s.at[d], lz_r.at[d], z_peer(d))
    late = l_z[0]
    for j in range(1, N_Z):
        late = late + l_z[j]
    late = late / n_total
    opv[...] = given + dot_nt(dot_nt(inverse, late[:, 0:24]), inverse[:, 8:16])
    store_p = pltpu.make_async_copy(opv, op_hbm, out_sem.at[2])
    store_p.start()
    for copy in sends:
        copy.wait_send()
    store_b.wait()
    store_i.wait()
    store_p.wait()


def on_device(tiles, tile_row, tile_col, basis, basis_image, search, search_image, ritz_values):
    vmem, dma = pltpu.VMEM, pltpu.SemaphoreType.DMA
    n_off = N_XY - 1
    return tuple(pl.pallas_call(
        kernel,
        out_shape=(
            jax.ShapeDtypeStruct((24, 1024), F32),
            jax.ShapeDtypeStruct((24, 1024), F32),
            jax.ShapeDtypeStruct((24, 24), F32),
        ),
        in_specs=[pl.BlockSpec(memory_space=pl.ANY)] * 8,
        out_specs=[pl.BlockSpec(memory_space=pl.ANY)] * 3,
        scratch_shapes=[
            vmem((TILES, TILE, TILE), BF16),
            vmem((1, 1, TILES), jnp.int32),
            vmem((1, 1, TILES), jnp.int32),
            pltpu.SMEM((VECS,), F32),
            vmem((40, 1024), F32),
            vmem((24, 1024), F32),
            vmem((64, TILE), F32),
            vmem((TILES, N_COL * 8), BF16),
            vmem((N_COL * 8, TILES), BF16),
            vmem((TILES, N_ROW * 8), BF16),
            vmem((N_ROW * 8, TILES), BF16),
            vmem((TILES * VECS, TILE), F32),
            vmem((TILES * VECS, TILE), F32),
            vmem((N_ROW, 64, TILE), BF16),
            vmem((N_COL, 64, TILE), BF16),
            vmem((TILES * VECS, TILE), F32),
            vmem((TILES * VECS, TILE), F32),
            vmem((N_COL, 64, TILE), F32),
            vmem((N_ROW, 64, TILE), F32),
            vmem((N_COL, 64, TILE), BF16),
            vmem((2, N_Z, 64, TILE), BF16),
            vmem((2, 64, TILE), F32),
            vmem((64, TILE), F32),
            vmem((N_XY, 64, TILE), F32),
            vmem((N_XY, 64, TILE), BF16),
            vmem((N_XY, 64, TILE), BF16),
            vmem((24, 1024), F32),
            vmem((24, 1024), F32),
            vmem((24, 24), F32),
            vmem((2, 24, TILE), F32),
            vmem((N_XY, 24, TILE), F32),
            vmem((2, 24, TILE), F32),
            vmem((N_Z, 24, TILE), F32),
            vmem((2, VECS, TILE), F32),
            vmem((N_XY, VECS, TILE), F32),
            vmem((2, VECS, TILE), F32),
            vmem((N_Z, VECS, TILE), F32),
            dma((8,)), dma((3,)),
            dma((n_off,)), dma((n_off,)), dma((N_YH,)), dma((N_YH,)),
            dma((N_Z,)), dma((N_Z,)), dma((N_Z,)), dma((N_Z,)),
            dma((2, N_Z)), dma((2, N_Z)), dma(()), dma(()), dma((4,)), dma((4,)), dma((n_off,)), dma((n_off,)),
            dma(()), dma(()), dma((n_off,)), dma((n_off,)), dma(()), dma(()), dma((N_Z,)), dma((N_Z,)),
            dma(()), dma(()), dma((n_off,)), dma((n_off,)), dma(()), dma(()), dma((N_Z,)), dma((N_Z,)),
        ],
        compiler_params=pltpu.CompilerParams(
            collective_id=0, has_side_effects=True, vmem_limit_bytes=56 * 2**20
        ),
        name="step",
    )(tiles, tile_row, tile_col, basis, basis_image, search, search_image, ritz_values))


def solution(mesh):
    vectors = P(None, ("row", "col"))
    return jax.shard_map(
        on_device,
        mesh=mesh,
        in_specs=(
            P("row", "col", None, None, None),
            P("row", "col", None),
            P("row", "col", None),
            vectors, vectors, vectors, vectors,
            P(),
        ),
        out_specs=(vectors, vectors, P()),
        check_vma=False,
    )
```

time: 491 us -> 81.3 us (0.17)
  the two profiles are of different devices: /device:TPU:1 before, /device:TPU:8 now
where the time goes in v1:
time: 81.3 us; the launch traced here: 81.1 us
  Pallas kernels  76.1 us (94%)
  local copies, waits for them, and re-layouts  4.38 us (5%)
    pallas_call x1, Pallas kernels, on_device(): pl.pallas_call(kernel, out_shape=(jax.ShapeDtypeStruct((24, 1024), F32),...  76.1 us
    unnamed x3, local copies, waits for them, and re-layouts  4.38 us

profile of v1, /device:TPU:8, one launch (start us, length us, event | category | flops | bytes accessed | tf_op | source)
XLA Modules:
  0.0 81.1 jit_solution(387483117166467869)
XLA Ops:
  0.6 76.1 %step.1 = (f32[24,1024]{1,0:T(8,128)}, f32[24,1024]{1,0:T(8,128)}, f32[24,24]{1,0:T(8,128)}) custom-call(bf16[1,1,128,128,128]{4,3,2,1,0:T(8,128)(2,1)} %tiles_hbm.1, s32[1,1,128]{2,1,0:T(1,128)} %row_hbm.1, s32[1,1,128]{2,1,0:T(1,128)} %col_hbm.1, f32[8,1024]{1,0:T(8,128)} %basis_hbm.1, f32[8,1024]{1,0:T(8,128)} %image_hbm.1, f32[8,1024]{1,0:T(8,128)} %search_hbm.1, ...), custom_call_target="tpu_custom_call" | custom-call | tf_op jit(solution)/shard_map/step/pallas_call | solution.py:350
  76.7 1.5 %copy.14 = f32[24,1024]{1,0:T(8,128)} copy(f32[24,1024]{1,0:T(8,128)} %get-tuple-element.6) | data formatting | bytes 196608
  78.3 1.5 %copy.15 = f32[24,1024]{1,0:T(8,128)} copy(f32[24,1024]{1,0:T(8,128)} %get-tuple-element.7) | data formatting | bytes 196608
  79.8 1.3 %copy.16 = f32[24,24]{1,0:T(8,128)} copy(f32[24,24]{1,0:T(8,128)} %get-tuple-element.8) | data formatting | bytes 4608

commit v2 on v1

v2 whole, which is shorter than its diff:
```python
import jax
import jax.numpy as jnp
from jax import lax
from jax.experimental import pallas as pl
from jax.experimental.pallas import tpu as pltpu
from jax.sharding import PartitionSpec as P

MESH = pl.DeviceIdType.MESH
TILE = 128
VECS = 8
TILES = 128
N_YH, N_X, N_Z = 4, 4, 12
N_XY = N_YH * N_X
N_ROW, N_COL = 2 * N_XY, 2 * N_Z
F32 = jnp.float32
BF16 = jnp.bfloat16
HIGHEST = lax.Precision.HIGHEST
NT = (((1,), (1,)), ((), ()))
NN = (((1,), (0,)), ((), ()))
Z_ORDER = (6, 5, 7, 4, 8, 3, 9, 2, 10, 1, 11)
OFFSETS = tuple((dy, dx) for dy in range(N_YH) for dx in range(N_X))[1:]


def dot_nt(left, right):
    return lax.dot_general(left, right, NT, precision=HIGHEST, preferred_element_type=F32)


def dot_nn(left, right):
    return lax.dot_general(left, right, NN, precision=HIGHEST, preferred_element_type=F32)


def matmul(left, right, dims):
    return lax.dot_general(left, right, dims, preferred_element_type=F32)


def halves(values):
    high = values.astype(BF16)
    return high, (values - high.astype(F32)).astype(BF16)


def slots_of(index, groups):
    piece, within = index // 8, index % 8
    return ((piece % 2) * groups + piece // 2) * 8 + within


def onehots(ahead, across, slots, count):
    column = jnp.transpose(jnp.broadcast_to(slots.astype(F32), (TILES, TILES)))
    lane = lax.broadcasted_iota(jnp.int32, (TILES, count), 1).astype(F32)
    ahead[...] = (lane == jnp.concatenate([column, column], axis=1)[:, :count]).astype(F32).astype(BF16)
    across[...] = (lax.broadcasted_iota(jnp.int32, (count, TILES), 0) == slots).astype(F32).astype(BF16)


def pick(picked, pieces, ahead, count):
    for m in range(VECS // 2):
        pair = pieces[:, 16 * m:16 * m + 16, :].astype(F32)
        even = pair[:, 0:8, :].reshape(count, TILE).astype(BF16)
        odd = pair[:, 8:16, :].reshape(count, TILE).astype(BF16)
        chosen = matmul(ahead[...], jnp.concatenate([even, odd], axis=1), NN)
        picked[pl.ds(2 * m, TILES, stride=VECS), :] = chosen[:, :TILE]
        picked[pl.ds(2 * m + 1, TILES, stride=VECS), :] = chosen[:, TILE:]


def place(terms, products, across, count):
    left = jnp.concatenate([across[...], across[...]], axis=1)
    for v in range(0, VECS, 2):
        columns = []
        for u in (v, v + 1):
            columns.append(jnp.concatenate(halves(products[pl.ds(u, TILES, stride=VECS), :]), axis=0))
        total = matmul(left, jnp.concatenate(columns, axis=1), NN)
        terms[:, 8 * v:8 * v + 8, :] = total[:, :TILE].reshape(count // 8, 8, TILE)
        terms[:, 8 * v + 8:8 * v + 16, :] = total[:, TILE:].reshape(count // 8, 8, TILE)


def multiply(products, picked, blocks):
    upper = lax.broadcasted_iota(jnp.int32, (16, TILE), 0) < 8

    def step(i, carry):
        for u in range(32):
            k = (i * 32 + u) * 2
            at = pl.ds(pl.multiple_of(k * 8, 16), 16)
            vectors = picked[at, :]
            left = jnp.concatenate(
                [jnp.where(upper, vectors, 0.0), jnp.where(upper, 0.0, vectors)], axis=1
            ).astype(BF16)
            products[at, :] = matmul(left, blocks[pl.ds(k, 2)].reshape(2 * TILE, TILE), NN)
        return carry

    lax.fori_loop(0, TILES // 64, step, 0)


def with_stack(sums, others, own):
    left, first, second = [], [], []
    for p in range(sums.shape[0]):
        for t in range(8):
            left.append(jnp.concatenate(halves(sums[p, pl.ds(t, VECS, stride=8), :]), axis=0))
            first.append(others[p, 16 * t:16 * t + 16, :])
            second.append(own[p, 8 * t:8 * t + 8, :].astype(BF16))
    left = jnp.concatenate(left, axis=1)
    first = matmul(left, jnp.concatenate(first, axis=1), NT)
    second = matmul(left, jnp.concatenate(second, axis=1), NT)
    both = jnp.concatenate([first, second], axis=1)
    return both[0:8] + both[8:16]


def by_tile(out, pieces, scratch):
    for p in range(out.shape[0]):
        scratch[...] = pieces[p].astype(F32)
        for t in range(8):
            out[p, 8 * t:8 * t + 8, :] = scratch[pl.ds(t, VECS, stride=8), :]


def kernel(
    tiles_hbm, row_hbm, col_hbm, basis_hbm, image_hbm, search_hbm, simage_hbm, ritz_hbm,
    ob, oi, opv,
    tiles, turned, row_v, col_v, ritz_s, work, images, pieces, scratch,
    ahead_r, across_r, ahead_c, across_c, picked, products,
    colbuf, rowbuf, others_c, others_r, own_c, own_r,
    rowterms, colterms, rowlow, ysib, rowsum, zlow, zr, csib, colsum, clow, cr,
    g_core, g_xy, g_yl, g_z, l_core, l_xy, l_yl, l_z,
    in_sem,
    cA_s, cA_r, cB_s, cB_r, zA_s, zA_r, yB_s, yB_r,
    oz_s, oz_r, oy_s, oy_r, ox_s, ox_r,
    ry_s, ry_r, rz_s, rz_r, sc_s, sc_r, sx_s, sx_r,
    gc_s, gc_r, gx_s, gx_r, gy_s, gy_r, gz_s, gz_r,
    lc_s, lc_r, lx_s, lx_r, ly_s, ly_r, lz_s, lz_r,
):
    row = lax.axis_index("row")
    col = lax.axis_index("col")
    xy, core = row // 2, row % 2
    yh, x = xy // N_X, xy % N_X
    z, yl = col // 2, col % 2
    sibling = (xy * 2 + 1 - core, col)
    across = (row, z * 2 + 1 - yl)

    def plane(dy, dx):
        return ((yh + dy) % N_YH) * N_X + (x + dx) % N_X

    def z_at(d):
        return (z + d) % N_Z

    def z_peer(d):
        return (row, z_at(d) * 2 + yl)

    def xy_peer(o):
        return (plane(*o) * 2 + core, col)

    def xy_from(o):
        return plane(N_YH - o[0], N_X - o[1])

    barrier = pltpu.get_barrier_semaphore()
    everyone = [z_peer(d) for d in Z_ORDER] + [xy_peer(o) for o in OFFSETS] + [sibling, across]
    for peer in everyone:
        pl.semaphore_signal(barrier, inc=1, device_id=peer, device_id_type=MESH)

    loads = [
        pltpu.make_async_copy(basis_hbm, work.at[pl.ds(0, 8)], in_sem.at[0]),
        pltpu.make_async_copy(image_hbm, work.at[pl.ds(24, 8)], in_sem.at[1]),
        pltpu.make_async_copy(ritz_hbm, ritz_s, in_sem.at[2]),
        pltpu.make_async_copy(search_hbm, work.at[pl.ds(16, 8)], in_sem.at[3]),
        pltpu.make_async_copy(simage_hbm, work.at[pl.ds(32, 8)], in_sem.at[4]),
        pltpu.make_async_copy(row_hbm, row_v, in_sem.at[5]),
        pltpu.make_async_copy(col_hbm, col_v, in_sem.at[6]),
        pltpu.make_async_copy(tiles_hbm.at[0, 0], tiles, in_sem.at[7]),
    ]
    for load in loads:
        load.start()
    for load in loads[:4]:
        load.wait()
    v_index = lax.broadcasted_iota(jnp.int32, (VECS, 1), 0)
    ritz = jnp.zeros((VECS, 1), F32)
    for v in range(VECS):
        ritz = jnp.where(v_index == v, ritz_s[v], ritz)
    residual = work[24:32, :] - ritz * work[0:8, :]
    work[8:16, :] = residual
    mine_col = core * N_XY + xy
    mine_row = yl * N_Z + z
    for t in range(8):
        cut = slice(t * TILE, (t + 1) * TILE)
        pieces[pl.ds(t, VECS, stride=8), :] = residual[:, cut]
        pair = jnp.concatenate([work[0:8, cut], work[16:24, cut]], axis=0).astype(BF16)
        others_c[xy, 16 * t:16 * t + 16, :] = pair
        others_r[z, 16 * t:16 * t + 16, :] = pair
    lowered = pieces[...].astype(BF16)
    colbuf[mine_col] = lowered
    rowbuf[mine_row] = lowered

    pl.semaphore_wait(barrier, len(everyone))

    sends = []

    def remote(src, dst, ss, rs, peer):
        return pltpu.make_async_remote_copy(
            src_ref=src, dst_ref=dst, send_sem=ss, recv_sem=rs, device_id=peer, device_id_type=MESH
        )

    def send(src, dst, ss, rs, peer):
        copy = remote(src, dst, ss, rs, peer)
        copy.start()
        sends.append(copy)

    def arrived(dst, ss, rs, peer):
        remote(dst, dst, ss, rs, peer).wait_recv()

    for d in Z_ORDER:
        send(rowbuf.at[mine_row], rowbuf.at[mine_row], zA_s.at[d], zA_r.at[d], z_peer(d))
    for j, o in enumerate(OFFSETS):
        send(colbuf.at[mine_col], colbuf.at[mine_col], cA_s.at[j], cA_r.at[j], xy_peer(o))
    send(rowbuf.at[mine_row], rowbuf.at[mine_row], yB_s.at[0], yB_r.at[0], across)

    def others_start():
        for d in Z_ORDER:
            send(others_r.at[z], others_r.at[z], oz_s.at[d], oz_r.at[d], z_peer(d))
        for d in (2, 1, 3):
            send(others_c.at[xy], others_c.at[xy], oy_s.at[d], oy_r.at[d], xy_peer((d, 0)))
        for d in (2, 1, 3):
            send(others_c.at[xy], others_c.at[xy], ox_s.at[0, d], ox_r.at[0, d], xy_peer((0, d)))

    others_start()

    for load in loads[5:7]:
        load.wait()
    onehots(ahead_r, across_r, slots_of(row_v[0], N_Z), N_COL * 8)
    onehots(ahead_c, across_c, slots_of(col_v[0], N_XY), N_ROW * 8)

    loads[4].wait()
    given = dot_nt(work[0:24, :], work[0:40, :])
    g_core[core] = jnp.concatenate(
        [given[0:8], given[8:16], given[16:24], jnp.zeros((8, 8), F32)], axis=1
    )
    send(g_core.at[core], g_core.at[core], gc_s, gc_r, sibling)

    loads[7].wait()

    def turn(i, carry):
        for u in range(16):
            turned[i * 16 + u] = tiles[i * 16 + u].T
        return carry

    lax.fori_loop(0, TILES // 16, turn, 0)

    for dy in range(N_YH):
        for dx in range(N_X):
            if (dy, dx) != (0, 0):
                j = OFFSETS.index((dy, dx))
                arrived(colbuf.at[core * N_XY + xy_from((dy, dx))], cA_s.at[j], cA_r.at[j], xy_peer((dy, dx)))
        block = colbuf.at[pl.ds(core * N_XY + ((yh + N_YH - dy) % N_YH) * N_X, N_X)]
        send(block, block, cB_s.at[dy], cB_r.at[dy], sibling)
    for d in reversed(Z_ORDER):
        here = rowbuf.at[yl * N_Z + z_at(N_Z - d)]
        arrived(here, zA_s.at[d], zA_r.at[d], z_peer(d))
        send(here, here, yB_s.at[d], yB_r.at[d], across)

    def others_on():
        for d in (1, 3, 2):
            here = others_c.at[plane(N_YH - d, 0)]
            arrived(here, oy_s.at[d], oy_r.at[d], xy_peer((d, 0)))
            for e in (2, 1, 3):
                send(here, here, ox_s.at[d, e], ox_r.at[d, e], xy_peer((0, e)))

    others_on()
    arrived(g_core.at[1 - core], gc_s, gc_r, sibling)
    g_xy[xy] = g_core[0] + g_core[1]
    for j, o in enumerate(OFFSETS):
        send(g_xy.at[xy], g_xy.at[xy], gx_s.at[j], gx_r.at[j], xy_peer(o))

    for dy in range(N_YH):
        block = colbuf.at[pl.ds((1 - core) * N_XY + ((yh + N_YH - dy) % N_YH) * N_X, N_X)]
        arrived(block, cB_s.at[dy], cB_r.at[dy], sibling)
    pick(picked, colbuf, ahead_c, N_ROW * 8)
    multiply(products, picked, turned)
    place(rowterms, products, across_r, N_COL * 8)
    for q in range(2):
        half = pl.ds(q * N_Z // 2, N_Z // 2)
        rowlow[half] = rowterms[pl.ds((1 - yl) * N_Z + q * N_Z // 2, N_Z // 2)].astype(BF16)
        send(rowlow.at[half], ysib.at[half], ry_s.at[q], ry_r.at[q], across)

    for d in range(N_Z):
        arrived(rowbuf.at[(1 - yl) * N_Z + z_at(N_Z - d)], yB_s.at[d], yB_r.at[d], across)
    pick(picked, rowbuf, ahead_r, N_COL * 8)
    multiply(products, picked, tiles)
    place(colterms, products, across_c, N_ROW * 8)
    chunk = N_XY // 4
    for q in range(4):
        send(
            colterms.at[pl.ds((1 - core) * N_XY + q * chunk, chunk)],
            csib.at[pl.ds(q * chunk, chunk)], sc_s.at[q], sc_r.at[q], sibling,
        )

    for j, o in enumerate(OFFSETS):
        arrived(g_xy.at[xy_from(o)], gx_s.at[j], gx_r.at[j], xy_peer(o))
    total = g_xy[0]
    for j in range(1, N_XY):
        total = total + g_xy[j]
    g_yl[yl] = total
    send(g_yl.at[yl], g_yl.at[yl], gy_s, gy_r, across)
    by_tile(own_c, colbuf.at[pl.ds(core * N_XY, N_XY)], scratch)
    by_tile(own_r, rowbuf.at[pl.ds(yl * N_Z, N_Z)], scratch)

    for q in range(4):
        at = pl.ds(q * chunk, chunk)
        arrived(csib.at[at], sc_s.at[q], sc_r.at[q], sibling)
        both = colterms[pl.ds(core * N_XY + q * chunk, chunk)] + csib[at]
        colsum[at] = both
        clow[at] = both.astype(BF16)
    for j, o in enumerate(OFFSETS):
        send(clow.at[plane(*o)], cr.at[xy], sx_s.at[j], sx_r.at[j], xy_peer(o))
    arrived(g_yl.at[1 - yl], gy_s, gy_r, across)
    g_z[z] = g_yl[0] + g_yl[1]
    for d in Z_ORDER:
        send(g_z.at[z], g_z.at[z], gz_s.at[d], gz_r.at[d], z_peer(d))
    for q in range(2):
        half = pl.ds(q * N_Z // 2, N_Z // 2)
        arrived(ysib.at[half], ry_s.at[q], ry_r.at[q], across)
        both = rowterms[pl.ds(yl * N_Z + q * N_Z // 2, N_Z // 2)] + ysib[half].astype(F32)
        rowsum[half] = both
        zlow[half] = both.astype(BF16)
    for d in Z_ORDER:
        send(zlow.at[z_at(d)], zr.at[z], rz_s.at[d], rz_r.at[d], z_peer(d))
    for d in (1, 2, 3):
        for e in range(N_YH):
            arrived(others_c.at[plane(N_YH - e, N_X - d)], ox_s.at[e, d], ox_r.at[e, d], xy_peer((0, d)))
    in_plane = with_stack(colsum, others_c, own_c)
    for d in Z_ORDER:
        arrived(others_r.at[z_at(N_Z - d)], oz_s.at[d], oz_r.at[d], z_peer(d))
    l_core[core] = jnp.zeros((VECS, TILE), F32)
    l_core[core, :, 0:24] = in_plane + with_stack(rowsum, others_r, own_r)
    send(l_core.at[core], l_core.at[core], lc_s, lc_r, sibling)
    arrived(l_core.at[1 - core], lc_s, lc_r, sibling)
    l_xy[xy] = l_core[0] + l_core[1]
    for j, o in enumerate(OFFSETS):
        send(l_xy.at[xy], l_xy.at[xy], lx_s.at[j], lx_r.at[j], xy_peer(o))

    for d in Z_ORDER:
        arrived(g_z.at[z_at(N_Z - d)], gz_s.at[d], gz_r.at[d], z_peer(d))
    total = g_z[0]
    for j in range(1, N_Z):
        total = total + g_z[j]
    n_total = F32(1024 * N_ROW * N_COL)
    total = total / n_total
    total = jnp.concatenate([total[:, 0:40], total[:, 40:80], total[:, 80:120]], axis=0)
    rows = lax.broadcasted_iota(jnp.int32, (24, 24), 0)
    columns = lax.broadcasted_iota(jnp.int32, (24, 24), 1)
    matrix = jnp.concatenate([total[:, 0:24], jnp.where(rows == columns, F32(1.0), F32(0.0))], axis=1)
    index = lax.broadcasted_iota(jnp.int32, (24, 1), 0)
    for step in range(24):
        pivot = jnp.sqrt(matrix[step:step + 1, step:step + 1])
        scaled = matrix[step:step + 1, :] / pivot
        factor = matrix[:, step:step + 1] / pivot
        matrix = jnp.where(
            index == step, scaled, jnp.where(index > step, matrix - factor * scaled, matrix)
        )
    inverse = matrix[:, 24:48]
    reordered = jnp.concatenate([inverse[:, 0:8], inverse[:, 16:24], inverse[:, 8:16]], axis=1)
    given = dot_nt(dot_nn(inverse, total[:, 24:32]), inverse[:, 0:8]) + dot_nt(
        dot_nn(inverse, total[:, 32:40]), inverse[:, 16:24]
    )
    ob[...] = dot_nn(inverse, work[0:24, :])

    for j, o in enumerate(OFFSETS):
        arrived(l_xy.at[xy_from(o)], lx_s.at[j], lx_r.at[j], xy_peer(o))
    late = l_xy[0]
    for j in range(1, N_XY):
        late = late + l_xy[j]
    l_yl[yl] = late
    send(l_yl.at[yl], l_yl.at[yl], ly_s, ly_r, across)
    arrived(l_yl.at[1 - yl], ly_s, ly_r, across)
    l_z[z] = l_yl[0] + l_yl[1]
    for d in Z_ORDER:
        send(l_z.at[z], l_z.at[z], lz_s.at[d], lz_r.at[d], z_peer(d))

    image = rowsum[z] + colsum[xy]
    for d in reversed(Z_ORDER):
        arrived(zr.at[z_at(N_Z - d)], rz_s.at[d], rz_r.at[d], z_peer(d))
        image = image + zr[z_at(N_Z - d)].astype(F32)
    for j, o in enumerate(OFFSETS):
        arrived(cr.at[xy_from(o)], sx_s.at[j], sx_r.at[j], xy_peer(o))
        image = image + cr[xy_from(o)].astype(F32)
    pieces[...] = image
    for t in range(8):
        images[8:16, t * TILE:(t + 1) * TILE] = pieces[pl.ds(t, VECS, stride=8), :]
    images[0:8, :] = work[24:32, :]
    images[16:24, :] = work[32:40, :]
    oi[...] = dot_nn(inverse, images[...])

    for d in Z_ORDER:
        arrived(l_z.at[z_at(N_Z - d)], lz_s.at[d], lz_r.at[d], z_peer(d))
    late = l_z[0]
    for j in range(1, N_Z):
        late = late + l_z[j]
    late = late / n_total
    opv[...] = given + dot_nt(dot_nt(reordered, late[:, 0:24]), inverse[:, 8:16])
    for copy in sends:
        copy.wait_send()


def on_device(tiles, tile_row, tile_col, basis, basis_image, search, search_image, ritz_values):
    vmem, dma = pltpu.VMEM, pltpu.SemaphoreType.DMA
    n_off = N_XY - 1
    outs = (
        jax.ShapeDtypeStruct((24, 1024), F32),
        jax.ShapeDtypeStruct((24, 1024), F32),
        jax.ShapeDtypeStruct((24, 24), F32),
    )

    def pairs(*shapes):
        return [dma(shape) for shape in shapes for _ in range(2)]

    results = pl.pallas_call(
        kernel,
        out_shape=tuple(vmem(out.shape, F32) for out in outs),
        in_specs=[pl.BlockSpec(memory_space=pl.ANY)] * 8,
        out_specs=[pl.BlockSpec(memory_space=vmem)] * 3,
        scratch_shapes=[
            vmem((TILES, TILE, TILE), BF16),
            vmem((TILES, TILE, TILE), BF16),
            vmem((1, 1, TILES), jnp.int32),
            vmem((1, 1, TILES), jnp.int32),
            pltpu.SMEM((VECS,), F32),
            vmem((40, 1024), F32),
            vmem((24, 1024), F32),
            vmem((64, TILE), F32),
            vmem((64, TILE), F32),
            vmem((TILES, N_COL * 8), BF16),
            vmem((N_COL * 8, TILES), BF16),
            vmem((TILES, N_ROW * 8), BF16),
            vmem((N_ROW * 8, TILES), BF16),
            vmem((TILES * VECS, TILE), F32),
            vmem((TILES * VECS, TILE), F32),
            vmem((N_ROW, 64, TILE), BF16),
            vmem((N_COL, 64, TILE), BF16),
            vmem((N_XY, 128, TILE), BF16),
            vmem((N_Z, 128, TILE), BF16),
            vmem((N_XY, 64, TILE), F32),
            vmem((N_Z, 64, TILE), F32),
            vmem((N_COL, 64, TILE), F32),
            vmem((N_ROW, 64, TILE), F32),
            vmem((N_Z, 64, TILE), BF16),
            vmem((N_Z, 64, TILE), BF16),
            vmem((N_Z, 64, TILE), F32),
            vmem((N_Z, 64, TILE), BF16),
            vmem((N_Z, 64, TILE), BF16),
            vmem((N_XY, 64, TILE), F32),
            vmem((N_XY, 64, TILE), F32),
            vmem((N_XY, 64, TILE), BF16),
            vmem((N_XY, 64, TILE), BF16),
            vmem((2, 8, TILE), F32),
            vmem((N_XY, 8, TILE), F32),
            vmem((2, 8, TILE), F32),
            vmem((N_Z, 8, TILE), F32),
            vmem((2, 8, TILE), F32),
            vmem((N_XY, 8, TILE), F32),
            vmem((2, 8, TILE), F32),
            vmem((N_Z, 8, TILE), F32),
            dma((8,)),
        ] + pairs(
            (n_off,), (N_YH,), (N_Z,), (N_Z,), (N_Z,), (N_YH,), (N_YH, N_X),
            (2,), (N_Z,), (4,), (n_off,),
            (), (n_off,), (), (N_Z,), (), (n_off,), (), (N_Z,),
        ),
        compiler_params=pltpu.CompilerParams(
            collective_id=0, has_side_effects=True, vmem_limit_bytes=56 * 2**20
        ),
        name="step",
    )(tiles, tile_row, tile_col, basis, basis_image, search, search_image, ritz_values)
    return tuple(results)


def solution(mesh):
    vectors = P(None, ("row", "col"))
    return jax.shard_map(
        on_device,
        mesh=mesh,
        in_specs=(
            P("row", "col", None, None, None),
            P("row", "col", None),
            P("row", "col", None),
            vectors, vectors, vectors, vectors,
            P(),
        ),
        out_specs=(vectors, vectors, P()),
        check_vma=False,
    )
```

time: 81.3 us -> 67.3 us (0.83)
  the two profiles are of different devices: /device:TPU:8 before, /device:TPU:2 now
where the time goes in v2:
time: 67.3 us; the launch traced here: 67.2 us
  Pallas kernels  64.7 us (96%)
  local copies, waits for them, and re-layouts  1.88 us (3%)
    pallas_call x1, Pallas kernels, on_device(): pl.pallas_call(kernel, out_shape=tuple((vmem(out.shape, F32) for out in o...  64.7 us
    unnamed x3, local copies, waits for them, and re-layouts  1.88 us

profile of v2, /device:TPU:2, one launch (start us, length us, event | category | flops | bytes accessed | tf_op | source)
XLA Modules:
  0.0 67.2 jit_solution(17016052463259353237)
XLA Ops:
  0.6 64.7 %step.1 = (f32[24,1024]{1,0:T(8,128)S(1)}, f32[24,1024]{1,0:T(8,128)S(1)}, f32[24,24]{1,0:T(8,128)S(1)}) custom-call(bf16[1,1,128,128,128]{4,3,2,1,0:T(8,128)(2,1)} %tiles_hbm.1, s32[1,1,128]{2,1,0:T(1,128)} %row_hbm.1, s32[1,1,128]{2,1,0:T(1,128)} %col_hbm.1, f32[8,1024]{1,0:T(8,128)} %basis_hbm.1, f32[8,1024]{1,0:T(8,128)} %image_hbm.1, ...), custom_call_target="tpu_custom_call" | custom-call | tf_op jit(solution)/shard_map/step/pallas_call | solution.py:408
  65.3 0.6 copy.14
  66.0 0.6 copy.16
  66.6 0.6 copy.15

commit v3 on v2

--- a/solution.py
+++ b/solution.py
@@ -18,6 +18,7 @@
 NT = (((1,), (1,)), ((), ()))
 NN = (((1,), (0,)), ((), ()))
 Z_ORDER = (6, 5, 7, 4, 8, 3, 9, 2, 10, 1, 11)
+IN_COL = tuple((d, e) for d in Z_ORDER for e in (0, 1)) + ((0, 1),)
 OFFSETS = tuple((dy, dx) for dy in range(N_YH) for dx in range(N_X))[1:]
 
 
@@ -102,6 +103,33 @@
     return both[0:8] + both[8:16]
 
 
+def pack(values):
+    line = lax.broadcasted_iota(jnp.int32, (VECS, TILE), 0) % 4
+    moved = jnp.where(line == 0, values, 0.0)
+    for j in range(1, 4):
+        moved = moved + jnp.where(line == j, pltpu.roll(values, 32 * j, axis=1), 0.0)
+    return jnp.concatenate(
+        [jnp.sum(moved[0:4], axis=0, keepdims=True), jnp.sum(moved[4:8], axis=0, keepdims=True)], axis=0
+    )
+
+
+def unpack(values):
+    line = lax.broadcasted_iota(jnp.int32, (VECS, TILE), 0) % 4
+    spread = jnp.concatenate(
+        [jnp.broadcast_to(values[0:1], (4, TILE)), jnp.broadcast_to(values[1:2], (4, TILE))], axis=0
+    )
+    moved = jnp.where(line == 0, spread, 0.0)
+    for j in range(1, 4):
+        moved = moved + jnp.where(line == j, pltpu.roll(spread, TILE - 32 * j, axis=1), 0.0)
+    return moved
+
+
+def tree(terms):
+    while len(terms) > 1:
+        terms = [a + b for a, b in zip(terms[::2], terms[1::2])] + terms[len(terms) // 2 * 2:]
+    return terms[0]
+
+
 def by_tile(out, pieces, scratch):
     for p in range(out.shape[0]):
         scratch[...] = pieces[p].astype(F32)
@@ -116,13 +144,13 @@
     ahead_r, across_r, ahead_c, across_c, picked, products,
     colbuf, rowbuf, others_c, others_r, own_c, own_r,
     rowterms, colterms, rowlow, ysib, rowsum, zlow, zr, csib, colsum, clow, cr,
-    g_core, g_xy, g_yl, g_z, l_core, l_xy, l_yl, l_z,
+    g_core, g_xy, g_yl, g_z, l_row, l_col,
     in_sem,
     cA_s, cA_r, cB_s, cB_r, zA_s, zA_r, yB_s, yB_r,
-    oz_s, oz_r, oy_s, oy_r, ox_s, ox_r,
+    oz_s, oz_r, on_s, on_r, oy_s, oy_r, ox_s, ox_r,
     ry_s, ry_r, rz_s, rz_r, sc_s, sc_r, sx_s, sx_r,
     gc_s, gc_r, gx_s, gx_r, gy_s, gy_r, gz_s, gz_r,
-    lc_s, lc_r, lx_s, lx_r, ly_s, ly_r, lz_s, lz_r,
+    lr_s, lr_r, ll_s, ll_r,
 ):
     row = lax.axis_index("row")
     col = lax.axis_index("col")
@@ -148,7 +176,10 @@
         return plane(N_YH - o[0], N_X - o[1])
 
     barrier = pltpu.get_barrier_semaphore()
-    everyone = [z_peer(d) for d in Z_ORDER] + [xy_peer(o) for o in OFFSETS] + [sibling, across]
+    def col_peer(d, e):
+        return (row, z_at(d) * 2 + (yl ^ e))
+
+    everyone = [col_peer(d, e) for d, e in IN_COL] + [(row ^ d, col) for d in range(1, N_ROW)]
     for peer in everyone:
         pl.semaphore_signal(barrier, inc=1, device_id=peer, device_id_type=MESH)
 
@@ -208,7 +239,7 @@
     send(rowbuf.at[mine_row], rowbuf.at[mine_row], yB_s.at[0], yB_r.at[0], across)
 
     def others_start():
-        for d in Z_ORDER:
+        for d in (6, 3, 9):
             send(others_r.at[z], others_r.at[z], oz_s.at[d], oz_r.at[d], z_peer(d))
         for d in (2, 1, 3):
             send(others_c.at[xy], others_c.at[xy], oy_s.at[d], oy_r.at[d], xy_peer((d, 0)))
@@ -258,6 +289,13 @@
                 send(here, here, ox_s.at[d, e], ox_r.at[d, e], xy_peer((0, e)))
 
     others_on()
+    for d in (0, 3, 9, 6):
+        here = others_r.at[z_at(N_Z - d)]
+        if d:
+            arrived(here, oz_s.at[d], oz_r.at[d], z_peer(d))
+        for e in (1, N_Z - 1):
+            send(here, here, on_s.at[e // 2, d // 3], on_r.at[e // 2, d // 3], z_peer(e))
+
     arrived(g_core.at[1 - core], gc_s, gc_r, sibling)
     g_xy[xy] = g_core[0] + g_core[1]
     for j, o in enumerate(OFFSETS):
@@ -320,15 +358,19 @@
         for e in range(N_YH):
             arrived(others_c.at[plane(N_YH - e, N_X - d)], ox_s.at[e, d], ox_r.at[e, d], xy_peer((0, d)))
     in_plane = with_stack(colsum, others_c, own_c)
-    for d in Z_ORDER:
-        arrived(others_r.at[z_at(N_Z - d)], oz_s.at[d], oz_r.at[d], z_peer(d))
-    l_core[core] = jnp.zeros((VECS, TILE), F32)
-    l_core[core, :, 0:24] = in_plane + with_stack(rowsum, others_r, own_r)
-    send(l_core.at[core], l_core.at[core], lc_s, lc_r, sibling)
-    arrived(l_core.at[1 - core], lc_s, lc_r, sibling)
-    l_xy[xy] = l_core[0] + l_core[1]
-    for j, o in enumerate(OFFSETS):
-        send(l_xy.at[xy], l_xy.at[xy], lx_s.at[j], lx_r.at[j], xy_peer(o))
+    for d in (0, 3, 9, 6):
+        for e in (1, N_Z - 1):
+            arrived(others_r.at[z_at(2 * N_Z - d - e)], on_s.at[e // 2, d // 3], on_r.at[e // 2, d // 3], z_peer(e))
+    last = in_plane + with_stack(rowsum, others_r, own_r)
+    l_row[row] = pack(jnp.concatenate([last, jnp.zeros((VECS, TILE - 24), F32)], axis=1))
+    for d in range(1, N_ROW):
+        send(l_row.at[row], l_row.at[row], lr_s.at[d], lr_r.at[d], (row ^ d, col))
+
+    for d in range(1, N_ROW):
+        arrived(l_row.at[row ^ d], lr_s.at[d], lr_r.at[d], (row ^ d, col))
+    l_col[col] = tree([l_row[j] for j in range(N_ROW)])
+    for d, e in IN_COL:
+        send(l_col.at[col], l_col.at[col], ll_s.at[d, e], ll_r.at[d, e], col_peer(d, e))
 
     for d in Z_ORDER:
         arrived(g_z.at[z_at(N_Z - d)], gz_s.at[d], gz_r.at[d], z_peer(d))
@@ -356,18 +398,6 @@
     )
     ob[...] = dot_nn(inverse, work[0:24, :])
 
-    for j, o in enumerate(OFFSETS):
-        arrived(l_xy.at[xy_from(o)], lx_s.at[j], lx_r.at[j], xy_peer(o))
-    late = l_xy[0]
-    for j in range(1, N_XY):
-        late = late + l_xy[j]
-    l_yl[yl] = late
-    send(l_yl.at[yl], l_yl.at[yl], ly_s, ly_r, across)
-    arrived(l_yl.at[1 - yl], ly_s, ly_r, across)
-    l_z[z] = l_yl[0] + l_yl[1]
-    for d in Z_ORDER:
-        send(l_z.at[z], l_z.at[z], lz_s.at[d], lz_r.at[d], z_peer(d))
-
     image = rowsum[z] + colsum[xy]
     for d in reversed(Z_ORDER):
         arrived(zr.at[z_at(N_Z - d)], rz_s.at[d], rz_r.at[d], z_peer(d))
@@ -382,12 +412,9 @@
     images[16:24, :] = work[32:40, :]
     oi[...] = dot_nn(inverse, images[...])
 
-    for d in Z_ORDER:
-        arrived(l_z.at[z_at(N_Z - d)], lz_s.at[d], lz_r.at[d], z_peer(d))
-    late = l_z[0]
-    for j in range(1, N_Z):
-        late = late + l_z[j]
-    late = late / n_total
+    for d, e in IN_COL:
+        arrived(l_col.at[z_at(N_Z - d) * 2 + (yl ^ e)], ll_s.at[d, e], ll_r.at[d, e], col_peer(d, e))
+    late = unpack(tree([l_col[j] for j in range(N_COL)])) / n_total
     opv[...] = given + dot_nt(dot_nt(reordered, late[:, 0:24]), inverse[:, 8:16])
     for copy in sends:
         copy.wait_send()
@@ -447,15 +474,13 @@
             vmem((N_XY, 8, TILE), F32),
             vmem((2, 8, TILE), F32),
             vmem((N_Z, 8, TILE), F32),
-            vmem((2, 8, TILE), F32),
-            vmem((N_XY, 8, TILE), F32),
-            vmem((2, 8, TILE), F32),
-            vmem((N_Z, 8, TILE), F32),
+            vmem((N_ROW, 2, TILE), F32),
+            vmem((N_COL, 2, TILE), F32),
             dma((8,)),
         ] + pairs(
-            (n_off,), (N_YH,), (N_Z,), (N_Z,), (N_Z,), (N_YH,), (N_YH, N_X),
+            (n_off,), (N_YH,), (N_Z,), (N_Z,), (N_Z,), (6, 4), (N_YH,), (N_YH, N_X),
             (2,), (N_Z,), (4,), (n_off,),
-            (), (n_off,), (), (N_Z,), (), (n_off,), (), (N_Z,),
+            (), (n_off,), (), (N_Z,), (N_ROW,), (N_Z, 2),
         ),
         compiler_params=pltpu.CompilerParams(
             collective_id=0, has_side_effects=True, vmem_limit_bytes=56 * 2**20

time: 67.3 us -> 65 us (0.966)
  the two profiles are of different devices: /device:TPU:2 before, /device:TPU:1 now
where the time goes in v3:
time: 65 us; the launch traced here: 64.8 us
  Pallas kernels  62.3 us (96%)
  local copies, waits for them, and re-layouts  1.88 us (3%)
    pallas_call x1, Pallas kernels, on_device(): pl.pallas_call(kernel, out_shape=tuple((vmem(out.shape, F32) for out in o...  62.3 us
    unnamed x3, local copies, waits for them, and re-layouts  1.88 us

profile of v3, /device:TPU:1, one launch (start us, length us, event | category | flops | bytes accessed | tf_op | source)
XLA Modules:
  0.0 64.8 jit_solution(16943743933213475193)
XLA Ops:
  0.6 62.3 %step.1 = (f32[24,1024]{1,0:T(8,128)S(1)}, f32[24,1024]{1,0:T(8,128)S(1)}, f32[24,24]{1,0:T(8,128)S(1)}) custom-call(bf16[1,1,128,128,128]{4,3,2,1,0:T(8,128)(2,1)} %tiles_hbm.1, s32[1,1,128]{2,1,0:T(1,128)} %row_hbm.1, s32[1,1,128]{2,1,0:T(1,128)} %col_hbm.1, f32[8,1024]{1,0:T(8,128)} %basis_hbm.1, f32[8,1024]{1,0:T(8,128)} %image_hbm.1, ...), custom_call_target="tpu_custom_call" | custom-call | tf_op jit(solution)/shard_map/step/pallas_call | solution.py:435
  62.9 0.6 copy.14
  63.6 0.6 copy.16
  64.2 0.6 copy.15

commit v4 on v3

--- a/solution.py
+++ b/solution.py
@@ -324,13 +324,6 @@
             csib.at[pl.ds(q * chunk, chunk)], sc_s.at[q], sc_r.at[q], sibling,
         )
 
-    for j, o in enumerate(OFFSETS):
-        arrived(g_xy.at[xy_from(o)], gx_s.at[j], gx_r.at[j], xy_peer(o))
-    total = g_xy[0]
-    for j in range(1, N_XY):
-        total = total + g_xy[j]
-    g_yl[yl] = total
-    send(g_yl.at[yl], g_yl.at[yl], gy_s, gy_r, across)
     by_tile(own_c, colbuf.at[pl.ds(core * N_XY, N_XY)], scratch)
     by_tile(own_r, rowbuf.at[pl.ds(yl * N_Z, N_Z)], scratch)
 
@@ -342,10 +335,6 @@
         clow[at] = both.astype(BF16)
     for j, o in enumerate(OFFSETS):
         send(clow.at[plane(*o)], cr.at[xy], sx_s.at[j], sx_r.at[j], xy_peer(o))
-    arrived(g_yl.at[1 - yl], gy_s, gy_r, across)
-    g_z[z] = g_yl[0] + g_yl[1]
-    for d in Z_ORDER:
-        send(g_z.at[z], g_z.at[z], gz_s.at[d], gz_r.at[d], z_peer(d))
     for q in range(2):
         half = pl.ds(q * N_Z // 2, N_Z // 2)
         arrived(ysib.at[half], ry_s.at[q], ry_r.at[q], across)
@@ -354,6 +343,13 @@
         zlow[half] = both.astype(BF16)
     for d in Z_ORDER:
         send(zlow.at[z_at(d)], zr.at[z], rz_s.at[d], rz_r.at[d], z_peer(d))
+    for j, o in enumerate(OFFSETS):
+        arrived(g_xy.at[xy_from(o)], gx_s.at[j], gx_r.at[j], xy_peer(o))
+    total = g_xy[0]
+    for j in range(1, N_XY):
+        total = total + g_xy[j]
+    g_yl[yl] = total
+    send(g_yl.at[yl], g_yl.at[yl], gy_s, gy_r, across)
     for d in (1, 2, 3):
         for e in range(N_YH):
             arrived(others_c.at[plane(N_YH - e, N_X - d)], ox_s.at[e, d], ox_r.at[e, d], xy_peer((0, d)))
@@ -366,6 +362,10 @@
     for d in range(1, N_ROW):
         send(l_row.at[row], l_row.at[row], lr_s.at[d], lr_r.at[d], (row ^ d, col))
 
+    arrived(g_yl.at[1 - yl], gy_s, gy_r, across)
+    g_z[z] = g_yl[0] + g_yl[1]
+    for d in Z_ORDER:
+        send(g_z.at[z], g_z.at[z], gz_s.at[d], gz_r.at[d], z_peer(d))
     for d in range(1, N_ROW):
         arrived(l_row.at[row ^ d], lr_s.at[d], lr_r.at[d], (row ^ d, col))
     l_col[col] = tree([l_row[j] for j in range(N_ROW)])

time: 65 us -> 64.9 us (level)
  no operation moved by 1% of the time
where the time goes in v4:
time: 64.9 us; the launch traced here: 64.7 us
  Pallas kernels  62.2 us (96%)
  local copies, waits for them, and re-layouts  1.88 us (3%)
    pallas_call x1, Pallas kernels, on_device(): pl.pallas_call(kernel, out_shape=tuple((vmem(out.shape, F32) for out in o...  62.2 us
    unnamed x3, local copies, waits for them, and re-layouts  1.88 us

profile of v4, /device:TPU:1, one launch (start us, length us, event | category | flops | bytes accessed | tf_op | source)
XLA Modules:
  0.0 64.7 jit_solution(6075945325289918136)
XLA Ops:
  0.6 62.2 %step.1 = (f32[24,1024]{1,0:T(8,128)S(1)}, f32[24,1024]{1,0:T(8,128)S(1)}, f32[24,24]{1,0:T(8,128)S(1)}) custom-call(bf16[1,1,128,128,128]{4,3,2,1,0:T(8,128)(2,1)} %tiles_hbm.1, s32[1,1,128]{2,1,0:T(1,128)} %row_hbm.1, s32[1,1,128]{2,1,0:T(1,128)} %col_hbm.1, f32[8,1024]{1,0:T(8,128)} %basis_hbm.1, f32[8,1024]{1,0:T(8,128)} %image_hbm.1, ...), custom_call_target="tpu_custom_call" | custom-call | tf_op jit(solution)/shard_map/step/pallas_call | solution.py:435
  62.8 0.6 copy.14
  63.5 0.6 copy.16
  64.1 0.6 copy.15

commit v5 on v3

--- a/solution.py
+++ b/solution.py
@@ -346,6 +346,10 @@
     g_z[z] = g_yl[0] + g_yl[1]
     for d in Z_ORDER:
         send(g_z.at[z], g_z.at[z], gz_s.at[d], gz_r.at[d], z_peer(d))
+    for d in (1, 2, 3):
+        for e in range(N_YH):
+            arrived(others_c.at[plane(N_YH - e, N_X - d)], ox_s.at[e, d], ox_r.at[e, d], xy_peer((0, d)))
+    in_plane = with_stack(colsum, others_c, own_c)
     for q in range(2):
         half = pl.ds(q * N_Z // 2, N_Z // 2)
         arrived(ysib.at[half], ry_s.at[q], ry_r.at[q], across)
@@ -354,10 +358,6 @@
         zlow[half] = both.astype(BF16)
     for d in Z_ORDER:
         send(zlow.at[z_at(d)], zr.at[z], rz_s.at[d], rz_r.at[d], z_peer(d))
-    for d in (1, 2, 3):
-        for e in range(N_YH):
-            arrived(others_c.at[plane(N_YH - e, N_X - d)], ox_s.at[e, d], ox_r.at[e, d], xy_peer((0, d)))
-    in_plane = with_stack(colsum, others_c, own_c)
     for d in (0, 3, 9, 6):
         for e in (1, N_Z - 1):
             arrived(others_r.at[z_at(2 * N_Z - d - e)], on_s.at[e // 2, d // 3], on_r.at[e // 2, d // 3], z_peer(e))

time: 65 us -> 65 us (level)
  no operation moved by 1% of the time
where the time goes in v5:
time: 65 us; the launch traced here: 64.8 us
  Pallas kernels  62.3 us (96%)
  local copies, waits for them, and re-layouts  1.88 us (3%)
    pallas_call x1, Pallas kernels, on_device(): pl.pallas_call(kernel, out_shape=tuple((vmem(out.shape, F32) for out in o...  62.3 us
    unnamed x3, local copies, waits for them, and re-layouts  1.88 us

profile of v5, /device:TPU:1, one launch (start us, length us, event | category | flops | bytes accessed | tf_op | source)
XLA Modules:
  0.0 64.8 jit_solution(3691366894782861807)
XLA Ops:
  0.6 62.3 %step.1 = (f32[24,1024]{1,0:T(8,128)S(1)}, f32[24,1024]{1,0:T(8,128)S(1)}, f32[24,24]{1,0:T(8,128)S(1)}) custom-call(bf16[1,1,128,128,128]{4,3,2,1,0:T(8,128)(2,1)} %tiles_hbm.1, s32[1,1,128]{2,1,0:T(1,128)} %row_hbm.1, s32[1,1,128]{2,1,0:T(1,128)} %col_hbm.1, f32[8,1024]{1,0:T(8,128)} %basis_hbm.1, f32[8,1024]{1,0:T(8,128)} %image_hbm.1, ...), custom_call_target="tpu_custom_call" | custom-call | tf_op jit(solution)/shard_map/step/pallas_call | solution.py:435
  62.9 0.6 copy.14
  63.6 0.6 copy.16
  64.2 0.6 copy.15
